TPU v7x, 256 devices: a whole 4x4x8 slice. The times are simulated.
256 devices in a mesh: shard: 64 (over z, x, core), rep: 4 (over y).
Axes of the slice: x: 4, y: 4, z: 8, core: 2. Of those that a mesh axis runs over, the one named last changes fastest.
Arguments:
- embeddings: bfloat16 [131072, 1024], P(('shard', 'rep')), may hold values from -200 to 200
- doc_cluster: int32 [131072, 1], P(('shard', 'rep')), may hold values from 0 to 63; in each aligned block of 512 rows (0 to 511, 512 to 1023, ...) at most 16 rows name the same one
- doc_rank: int32 [131072], P(('shard', 'rep')), may hold values from 0 to 131071, each once
Outputs:
- best_similarity: float32 [131072], P(('shard', 'rep'))
Inputs may be any that keep to these rules, and one draw needn't show every extreme that they name: `doc_cluster`: among the rows of one device no cluster is named more than 16 times, and some device names some cluster exactly 16 times. `doc_rank`: each rank is held by exactly one document.
All inputs are finite; a program needn't handle non-finite values.
Results may differ from a plain program's by a relative error of at most 0.00049.
Values may be sent and summed in bfloat16 or wider, within the bound.
A program may use at most 64 MiB of HBM per device.

v0:
```python
import jax
import jax.numpy as jnp
from jax import lax
from jax.sharding import PartitionSpec as P


def unit_rows(embed_rows):
    values = embed_rows.astype(jnp.float32)
    scale = lax.rsqrt(jnp.sum(values * values, axis=1, keepdims=True) + 1e-06)
    return (values * scale).astype(jnp.bfloat16)


def tile_pairs(left_rows, left_rank, right_rows, right_rank):
    left_count = left_rows.shape[0]
    right_count = right_rows.shape[0]
    left_tile = min(512, left_count)
    right_tile = min(512, right_count)
    column_best = [
        jnp.full((right_tile,), -1.0, jnp.float32) for col_step in range(right_count // right_tile)
    ]
    row_best = []
    for row_step in range(left_count // left_tile):
        tile_rows = left_rows[row_step * left_tile : (row_step + 1) * left_tile]
        tile_rank = left_rank[row_step * left_tile : (row_step + 1) * left_tile]
        running = jnp.full((left_tile,), -1.0, jnp.float32)
        for col_step in range(right_count // right_tile):
            other_rows = right_rows[col_step * right_tile : (col_step + 1) * right_tile]
            other_rank = right_rank[col_step * right_tile : (col_step + 1) * right_tile]
            active = jnp.any(tile_rank >= 0) & jnp.any(other_rank >= 0)

            def compute_tile():
                scores = lax.dot_general(
                    tile_rows,
                    other_rows,
                    (((1,), (1,)), ((), ())),
                    preferred_element_type=jnp.float32,
                )
                earlier = (other_rank[None, :] >= 0) & (other_rank[None, :] < tile_rank[:, None])
                later = (tile_rank[:, None] >= 0) & (tile_rank[:, None] < other_rank[None, :])
                return (
                    jnp.max(jnp.where(earlier, scores, -1.0), axis=1),
                    jnp.max(jnp.where(later, scores, -1.0), axis=0),
                )

            def skip_tile():
                return (
                    jnp.full((left_tile,), -1.0, jnp.float32),
                    jnp.full((right_tile,), -1.0, jnp.float32),
                )

            row_part, column_part = lax.cond(active, compute_tile, skip_tile)
            running = jnp.maximum(running, row_part)
            column_best[col_step] = jnp.maximum(column_best[col_step], column_part)
        row_best.append(running)
    return (jnp.concatenate(row_best), jnp.concatenate(column_best))


def on_device(embeddings, doc_cluster, doc_rank):
    doc_count = embeddings.shape[0]
    width = embeddings.shape[1]
    owners = lax.axis_size("shard")
    slots = 2 * doc_count // owners
    held = owners * slots
    unit = unit_rows(embeddings)
    target = doc_cluster[:, 0]
    member = (target[:, None] == jnp.arange(owners, dtype=jnp.int32)[None, :]).astype(jnp.int32)
    seat = jnp.sum((jnp.cumsum(member, axis=0) - member) * member, axis=1)
    destination = target * slots + seat
    outgoing = jnp.zeros((held, width), jnp.bfloat16).at[destination].set(unit)
    out_rank = jnp.full((held,), -1, jnp.int32).at[destination].set(doc_rank)
    arrived, arrived_rank = (
        lax.all_to_all(
            outgoing.reshape(owners, slots, width), "shard", split_axis=0, concat_axis=0, tiled=True
        ),
        lax.all_to_all(
            out_rank.reshape(owners, slots), "shard", split_axis=0, concat_axis=0, tiled=True
        ),
    )
    member_rows = arrived.reshape(held, width)
    member_rank = arrived_rank.reshape(held)
    valid = (member_rank >= 0).astype(jnp.int32)
    valid_count = jnp.sum(valid)
    placement = jnp.where(valid > 0, jnp.cumsum(valid) - 1, valid_count + jnp.cumsum(1 - valid) - 1)
    packed = jnp.zeros_like(member_rows).at[placement].set(member_rows)
    packed_rank = jnp.full((held,), -1, jnp.int32).at[placement].set(member_rank)
    piece_rows = lax.all_gather(packed, "rep", axis=0, tiled=True)
    piece_rank = lax.all_gather(packed_rank, "rep", axis=0, tiled=True)
    row_part, unused_part = tile_pairs(packed, packed_rank, piece_rows, piece_rank)
    packed_best = jnp.maximum(jnp.full((held,), -1.0, jnp.float32), row_part)
    slot_best = packed_best[placement].reshape(owners, slots)
    homeward = lax.all_to_all(slot_best, "shard", split_axis=0, concat_axis=0, tiled=True)
    return homeward.reshape(held)[destination]


def solution(mesh):
    placed = (P(("shard", "rep"), None), P(("shard", "rep"), None), P(("shard", "rep")))
    return jax.shard_map(
        on_device, mesh=mesh, in_specs=placed, out_specs=P(("shard", "rep")), check_vma=False
    )
```

profile of v0, /device:TPU:32, one launch (start us, length us, event | category | flops | bytes accessed | tf_op | source)
XLA Modules:
  0.0 258.1 jit_solution(8685743967497821665)
XLA Ops:
  6.5 0.8 fusion.27
  7.3 1.2 reduce-window.24
  8.8 0.8 fusion.26
  9.6 0.7 compare_select_fusion.1
  10.3 2.6 %scatter_custom_fusion = s32[1024]{0:T(1024)S(1)} fusion(s32[512]{0:T(512)S(1)} %bitcast.71, s32[512]{0:T(512)} %param.37, s32[]{:T(128)} %constant.138.clone.1), kind=kCustom, calls=%fused_computation.89 | custom fusion | bytes 4608 | tf_op jit(solution)/shard_map/scatter | solution.py:70
  12.9 0.7 all_to_all.15
  13.6 11.6 %all-to-all-start = ((s32[64,1,16]{2,1,0:T(1,128)}), s32[64,1,16]{2,1,0:T(1,128)S(1)}, u32[]{:S(2)}, u32[]{:S(2)}) async-start(s32[64,1,16]{2,1,0:T(1,128)} %bitcast.5), calls=%async_computation | async-start | bytes 65536 | tf_op jit(solution)/shard_map/all_to_all | solution.py:75
  25.2 1.5 fusion.16
  26.7 4.2 %scatter_custom_fusion.2 = bf16[1024,1024]{1,0:T(8,128)(2,1)} fusion(s32[512]{0:T(512)S(1)} %bitcast.72, bf16[512,1024]{1,0:T(8,128)(2,1)S(1)} %copy-done.1, f32[512]{0:T(512)S(1)} %add_rsqrt_fusion, bf16[]{:T(256)} %constant.133.clone.1), kind=kCustom, calls=%fused_computation.58 | custom fusion | flops 1572864 | bytes 3147778 | tf_op jit(solution)/shard_map/scatter | solution.py:69
  30.9 2.9 %all-to-all-done = s32[64,1,16]{2,1,0:T(1,128)S(1)} async-done(((s32[64,1,16]{2,1,0:T(1,128)}), s32[64,1,16]{2,1,0:T(1,128)S(1)}, u32[]{:S(2)}, u32[]{:S(2)}) %all-to-all-start) | async-done | bytes 4128 | tf_op jit(solution)/shard_map/all_to_all | solution.py:75
  33.8 7.4 %all-to-all-start.1 = ((bf16[64,16,1024]{2,1,0:T(8,128)(2,1)}), bf16[64,16,1024]{2,1,0:T(8,128)(2,1)S(1)}, u32[]{:S(2)}, u32[]{:S(2)}) async-start(bf16[64,16,1024]{2,1,0:T(8,128)(2,1)} %bitcast.9), calls=%async_computation.1 | async-start | bytes 4194304 | tf_op jit(solution)/shard_map/all_to_all | solution.py:72
  41.5 0.5 broadcast.380
  42.0 1.4 fusion.34
  43.5 0.3 reduce-window.26
  43.9 0.3 reduce-window.36
  44.6 0.7 add_add_fusion
  45.3 46.3 %all-to-all-done.1 = bf16[64,16,1024]{2,1,0:T(8,128)(2,1)S(1)} async-done(((bf16[64,16,1024]{2,1,0:T(8,128)(2,1)}), bf16[64,16,1024]{2,1,0:T(8,128)(2,1)S(1)}, u32[]{:S(2)}, u32[]{:S(2)}) %all-to-all-start.1) | async-done | bytes 2097184 | tf_op jit(solution)/shard_map/all_to_all | solution.py:72
  91.6 6.9 %scatter_custom_fusion.3 = bf16[1024,1024]{1,0:T(8,128)(2,1)} fusion(s32[1024]{0:T(1024)S(1)} %bitcast.65, bf16[1024,1024]{1,0:T(8,128)(2,1)S(1)} %bitcast.62, bf16[]{:T(256)} %constant.133.clone.1), kind=kCustom, calls=%fused_computation.60 | custom fusion | bytes 2097154 | tf_op jit(solution)/shard_map/scatter | solution.py:84
  98.6 4.3 %scatter_custom_fusion.1 = s32[1024]{0:T(1024)S(1)} fusion(s32[1024]{0:T(1024)S(1)} %bitcast.66, s32[1024]{0:T(1024)S(1)} %reshape.266, s32[]{:T(128)} %constant.138.clone.1), kind=kCustom, calls=%fused_computation.87 | custom fusion | bytes 4100 | tf_op jit(solution)/shard_map/scatter | solution.py:85
  102.9 12.5 %all_gather.6 = s32[4096]{0:T(1024)S(1)} all-gather(s32[1024]{0:T(1024)S(1)} %scatter_custom_fusion.1), channel_id=1, replica_groups=mesh['shard'=64,'rep'=4] {'rep'}, dimensions={0}, use_global_device_ids=true | all-gather | bytes 20480 | tf_op jit(solution)/shard_map/all_gather | solution.py:87
  115.4 0.7 compare_reduce_fusion.10
  116.1 0.8 compare_reduce_fusion.9
  137.3 1.6 fusion.36
  138.8 42.9 %all-gather.2.cloned.1.call-done = bf16[4096,1024]{1,0:T(8,128)(2,1)} async-done(((bf16[1024,1024]{1,0:T(8,128)(2,1)}), bf16[4096,1024]{1,0:T(8,128)(2,1)}) %all-gather.2.cloned.1.call-update) | async-done | bytes 8388624 | tf_op jit(solution)/shard_map/all_gather | solution.py:86
  181.7 5.7 %fusion.35 = (bf16[512,1024]{1,0:T(8,128)(2,1)S(1)}, bf16[512,1024]{1,0:T(8,128)(2,1)}, bf16[512,1024]{1,0:T(8,128)(2,1)}, bf16[512,1024]{1,0:T(8,128)(2,1)}, bf...) fusion(bf16[4096,1024]{1,0:T(8,128)(2,1)} %all-gather.2.cloned., ...), kind=kLoop, calls=%fused_computation.104 | loop fusion | bytes 16777216 | tf_op jit(solution)/shard_map/slice | solution.py:27
  187.5 2.4 conditional.31
  187.5 2.3 fusion.15
  189.8 2.4 conditional.30
  189.9 2.3 fusion.14
  192.2 2.4 conditional.29
  192.2 2.3 fusion.13
  194.6 2.4 conditional.28
  194.6 2.3 fusion.12
  197.0 2.4 conditional.27
  197.0 2.3 fusion.11
  199.3 2.0 conditional.26
  199.4 2.0 fusion.10
  201.4 2.1 conditional.25
  201.4 2.0 fusion.9
  203.4 2.1 conditional.24
  203.5 2.0 fusion.8
  205.5 2.4 conditional.23
  205.5 2.3 fusion.7
  207.9 2.4 conditional.22
  207.9 2.3 fusion.6
  210.2 2.4 conditional.21
  210.3 2.3 fusion.5
  212.6 2.4 conditional.20
  212.6 2.3 fusion.4
  215.0 2.4 conditional.19
  215.0 2.3 fusion.3
  217.4 2.3 conditional.18
  217.6 2.0 fusion.2
  219.6 2.1 conditional.17
  219.7 2.0 fusion.1
  221.7 2.1 conditional.16
  221.7 2.0 fusion
  223.8 4.5 %gather_fusion = f32[1024]{0:T(1024)S(1)} fusion(f32[1024]{0:T(1024)S(1)} %maximum_maximum_fusion, s32[1024]{0:T(1024)S(1)} %broadcast_clamp_fusion), kind=kCustom, calls=%fused_computation | custom fusion | bytes 12288 | tf_op jit(solution)/shard_map/gather | solution.py:90
  228.3 0.7 all_to_all.18
  229.0 8.9 %all-to-all-start.2 = ((f32[64,1,16]{2,1,0:T(1,128)}), f32[64,1,16]{2,1,0:T(1,128)S(1)}, u32[]{:S(2)}, u32[]{:S(2)}) async-start(f32[64,1,16]{2,1,0:T(1,128)} %bitcast.11), calls=%async_computation.2 | async-start | bytes 65536 | tf_op jit(solution)/shard_map/all_to_all | solution.py:91
  238.0 8.6 %all-to-all-done.2 = f32[64,1,16]{2,1,0:T(1,128)S(1)} async-done(((f32[64,1,16]{2,1,0:T(1,128)}), f32[64,1,16]{2,1,0:T(1,128)S(1)}, u32[]{:S(2)}, u32[]{:S(2)}) %all-to-all-start.2) | async-done | bytes 4128 | tf_op jit(solution)/shard_map/all_to_all | solution.py:91
  246.6 0.5 broadcast.381
  247.1 0.7 reduce.21
  247.9 3.4 %gather_fusion.1 = f32[512]{0:T(512)} fusion(f32[1024]{0:T(1024)S(1)} %reshape.236, s32[1024]{0:T(1024)S(1)} %pad_clamp_fusion), kind=kCustom, calls=%fused_computation.1 | custom fusion | bytes 6144 | tf_op jit(solution)/shard_map/gather | solution.py:92
  (46 shorter events, 1.4 us)
Async XLA Ops:
  6.5 20.2 %copy-start.1 = (bf16[512,1024]{1,0:T(8,128)(2,1)S(1)}, bf16[512,1024]{1,0:T(8,128)(2,1)}, u32[]{:S(2)}) copy-start(bf16[512,1024]{1,0:T(8,128)(2,1)} %param.35) | copy-start | bytes 3145732
  13.6 20.2 %all-to-all-start = ((s32[64,1,16]{2,1,0:T(1,128)}), s32[64,1,16]{2,1,0:T(1,128)S(1)}, u32[]{:S(2)}, u32[]{:S(2)}) async-start(s32[64,1,16]{2,1,0:T(1,128)} %bitcast.5), calls=%async_computation | async-start | bytes 65536 | tf_op jit(solution)/shard_map/all_to_all | solution.py:75
  33.8 57.9 %all-to-all-start.1 = ((bf16[64,16,1024]{2,1,0:T(8,128)(2,1)}), bf16[64,16,1024]{2,1,0:T(8,128)(2,1)S(1)}, u32[]{:S(2)}, u32[]{:S(2)}) async-start(bf16[64,16,1024]{2,1,0:T(8,128)(2,1)} %bitcast.9), calls=%async_computation.1 | async-start | bytes 4194304 | tf_op jit(solution)/shard_map/all_to_all | solution.py:72
  41.2 140.5 %all-gather.2.cloned.1.call-start = ((), (), s32[]{:S(2)}) async-start(), calls=%async_computation.3 | async-start | bytes 10485760 | tf_op jit(solution)/shard_map/all_gather | solution.py:86
  98.5 38.7 %copy-start = (bf16[1024,1024]{1,0:T(8,128)(2,1)S(1)}, bf16[1024,1024]{1,0:T(8,128)(2,1)}, u32[]{:S(2)}) copy-start(bf16[1024,1024]{1,0:T(8,128)(2,1)} %scatter_custom_fusion.3) | copy-start | bytes 6291460
  229.0 17.5 %all-to-all-start.2 = ((f32[64,1,16]{2,1,0:T(1,128)}), f32[64,1,16]{2,1,0:T(1,128)S(1)}, u32[]{:S(2)}, u32[]{:S(2)}) async-start(f32[64,1,16]{2,1,0:T(1,128)} %bitcast.11), calls=%async_computation.2 | async-start | bytes 65536 | tf_op jit(solution)/shard_map/all_to_all | solution.py:91
Sparse Core Ops, SparseCore 0:
  98.7 83.0 all-gather.1
where the time goes:
time: 262 us; the launch traced here: 258 us
  waiting for transfers between devices  101 us (39%)
  matrix products  35.5 us (14%)
  between operations  33.9 us (13%)
  local copies, waits for them, and re-layouts  32.4 us (12%)
  starting transfers between devices  28 us (11%)
  other arithmetic  14.6 us (6%)
  blocking collectives  12.5 us (5%)
    all_to_all x1, waiting for transfers between devices, on_device(): lax.all_to_all(outgoing.reshape(owners, slots, width), 'shard', split_axi...  46.3 us
    all_gather x1, waiting for transfers between devices, on_device(): piece_rows = lax.all_gather(packed, 'rep', axis=0, tiled=True)  42.9 us
    dot_general x16, matrix products, compute_tile(): lax.dot_general(tile_rows, other_rows, (((1,), (1,)), ((), ())), preferre...  35.5 us
    all_gather x1, blocking collectives, on_device(): piece_rank = lax.all_gather(packed_rank, 'rep', axis=0, tiled=True)  12.5 us
    all_to_all x1, starting transfers between devices, on_device(): lax.all_to_all(out_rank.reshape(owners, slots), 'shard', split_axis=0, co...  11.6 us
    all_to_all x1, starting transfers between devices, on_device(): lax.all_to_all(slot_best, 'shard', split_axis=0, concat_axis=0, tiled=True)  8.93 us
    all_to_all x1, waiting for transfers between devices, on_device(): lax.all_to_all(slot_best, 'shard', split_axis=0, concat_axis=0, tiled=True)  8.6 us
    all_to_all x1, starting transfers between devices, on_device(): lax.all_to_all(outgoing.reshape(owners, slots, width), 'shard', split_axi...  7.45 us
  transfers between devices with their start and end apart: 4, of which 4 were waited for; matrix products, arithmetic and copies ran while one was open for 7% of the time, Pallas kernels for 0%

commit v1 on v0

v1 whole, which is shorter than its diff:
```python
import functools
from types import SimpleNamespace

import jax
import jax.numpy as jnp
from jax import lax
from jax.experimental import pallas as pl
from jax.experimental.pallas import tpu as pltpu
from jax.sharding import PartitionSpec as P

SIZES = dict(Z=8, X=4, Y=4, K=2, SLOT=16)
MESH = pl.DeviceIdType.MESH
NONE_RANK = 2.0e9


def make_config(Z, X, Y, K, SLOT):
    return SimpleNamespace(
        Z=Z, X=X, Y=Y, K=K, SLOT=SLOT, XY=X * Y, J=X * K, W=X * Y * SLOT, YS=Y // K,
        order=[0] + [d for i in range(1, Z // 2) for d in (i, Z - i)] + [Z // 2],
    )


def kernel(
    cfg, emb_ref, cl_ref, rank_ref, out_ref,
    unit, hot, lane_hot, sbuf, relay, rows, rs, rz, rp, rkown, rksib, rj, res, ret1, ret2,
    z_send, z_recv, rz_send, rz_recv, p_send, p_recv, p_self, rp_send, rp_recv, rp_self,
    s_send, s_recv, rks_send, rks_recv, r1_send, r1_recv, r1_self, r2_send, r2_recv,
):
    Z, X, Y, K, SLOT, XY, J, W, YS = (
        cfg.Z, cfg.X, cfg.Y, cfg.K, cfg.SLOT, cfg.XY, cfg.J, cfg.W, cfg.YS
    )
    order = cfg.order
    n_docs, width = emb_ref.shape
    held = Z * J
    shard = lax.axis_index("shard")
    y = lax.axis_index("rep")
    k = shard % K
    x = (shard // K) % X
    z = shard // (K * X)
    p = x * Y + y
    owner = (y % YS) == (x % YS)
    j_self = jnp.where(owner, x * K + y // YS, -1)

    def dev(zz, xx, yy, kk):
        return ((zz * X + xx) * K + kk, yy)

    def dev_line(distance):
        return dev((z + distance) % Z, x, y, k)

    def dev_owner(j):
        xx = j // K
        return dev(z, xx, (j % K) * YS + xx % YS, k)

    def dev_member(q):
        return dev(z, q // Y, q % Y, k)

    sibling = dev(z, x, y, 1 - k)

    barrier = pltpu.get_barrier_semaphore()

    @pl.loop(1, Z)
    def _(i):
        pl.semaphore_signal(barrier, inc=1, device_id=dev_line(i), device_id_type=MESH)

    @pl.loop(0, J)
    def _(j):
        @pl.when(j != j_self)
        def _():
            pl.semaphore_signal(barrier, inc=1, device_id=dev_owner(j), device_id_type=MESH)

    @pl.when(owner)
    def _():
        @pl.loop(0, XY)
        def _(q):
            @pl.when(q != p)
            def _():
                pl.semaphore_signal(barrier, inc=1, device_id=dev_member(q), device_id_type=MESH)

        pl.semaphore_signal(barrier, inc=1, device_id=sibling, device_id_type=MESH)

    cl = cl_ref[...]
    log_j = J.bit_length() - 1
    away = (z - (cl >> log_j)) & (Z - 1)
    step = jnp.where(away == 0, 0, jnp.where(away <= Z // 2, 2 * away - 1, 2 * (Z - away)))
    rel = step * J + (cl & (J - 1))
    member = lax.broadcasted_iota(jnp.int32, (held, n_docs), 0) == rel
    hot_f = jnp.where(member, 1.0, 0.0)
    hot_b = hot_f.astype(jnp.bfloat16)
    hot[...] = hot_b
    before = (
        lax.broadcasted_iota(jnp.int32, (n_docs, n_docs), 0)
        < lax.broadcasted_iota(jnp.int32, (n_docs, n_docs), 1)
    )
    before_b = jnp.where(before, 1.0, 0.0).astype(jnp.bfloat16)
    prefix = jnp.dot(hot_b, before_b, preferred_element_type=jnp.float32)
    seat = jnp.sum(hot_f * prefix, axis=0, keepdims=True).astype(jnp.int32)
    place = rel * SLOT + seat
    lane = p * SLOT + seat
    lane_b = jnp.where(
        lax.broadcasted_iota(jnp.int32, (W, n_docs), 0) == lane, 1.0, 0.0
    ).astype(jnp.bfloat16)
    lane_hot[...] = lane_b

    rank1 = rank_ref[...] + 1
    parts = [(rank1 & 63), ((rank1 >> 6) & 63), (rank1 >> 12)]
    stacked = jnp.concatenate(
        [(hot_f * part.astype(jnp.float32)).astype(jnp.bfloat16) for part in parts], axis=0
    )
    spread = lax.dot_general(
        stacked, lane_b, (((1,), (1,)), ((), ())), preferred_element_type=jnp.float32
    )
    rank_rows = spread[:held] + 64.0 * spread[held : 2 * held] + 4096.0 * spread[2 * held :]
    for c in range(held):
        rs[c // J, c % J] = rank_rows[c : c + 1]

    block = min(64, n_docs)

    @pl.loop(0, n_docs // block)
    def _(i):
        at = pl.ds(pl.multiple_of(i * block, block), block)
        values = emb_ref[at].astype(jnp.float32)
        scale = lax.rsqrt(jnp.sum(values * values, axis=1, keepdims=True) + 1e-06)
        unit[at] = (values * scale).astype(jnp.bfloat16)

    def pack(n):
        slots = lax.broadcasted_iota(jnp.int32, (J * SLOT, n_docs), 0) + n * J * SLOT
        pick = jnp.where(slots == place, 1.0, 0.0).astype(jnp.bfloat16)
        got = jnp.dot(pick, unit[...], preferred_element_type=jnp.float32)
        return got.astype(jnp.bfloat16).reshape(J, SLOT, width)

    pl.semaphore_wait(
        barrier, jnp.where(owner, (Z - 1) + (J - 1) + (XY - 1) + 1, (Z - 1) + J)
    )

    def rank_copy(n):
        return pltpu.make_async_remote_copy(
            src_ref=rs.at[n], dst_ref=rz.at[n], send_sem=rz_send.at[n], recv_sem=rz_recv.at[n],
            device_id=dev_line(Z - order[n]), device_id_type=MESH,
        )

    def line_copy(n):
        return pltpu.make_async_remote_copy(
            src_ref=sbuf.at[n], dst_ref=relay.at[n], send_sem=z_send.at[n], recv_sem=z_recv.at[n],
            device_id=dev_line(Z - order[n]), device_id_type=MESH,
        )

    for n in range(1, Z):
        rank_copy(n).start()
    for n in range(1, Z):
        sbuf[n] = pack(n)
        line_copy(n).start()
    relay[0] = pack(0)
    rz[0] = rs[0]

    for n in range(1, Z):
        rank_copy(n).wait_recv()

    @pl.loop(0, J)
    def _(j):
        @pl.when(j != j_self)
        def _():
            pltpu.make_async_remote_copy(
                src_ref=rz.at[:, j], dst_ref=rp.at[p], send_sem=rp_send, recv_sem=rp_recv,
                device_id=dev_owner(j), device_id_type=MESH,
            ).start()

        @pl.when(j == j_self)
        def _():
            pltpu.make_async_copy(rz.at[:, j], rp.at[p], rp_self).start()

    def wait_bytes(ref, sem):
        pltpu.make_async_copy(ref, ref, sem).wait()

    def sib_copy(n):
        return pltpu.make_async_remote_copy(
            src_ref=rows.at[n, 0], dst_ref=rows.at[n, 1], send_sem=s_send.at[n],
            recv_sem=s_recv.at[n], device_id=sibling, device_id_type=MESH,
        )

    def rank_sib_copy():
        return pltpu.make_async_remote_copy(
            src_ref=rkown, dst_ref=rksib, send_sem=rks_send, recv_sem=rks_recv,
            device_id=sibling, device_id_type=MESH,
        )

    def forward(n):
        @pl.loop(0, J)
        def _(j):
            @pl.when(j != j_self)
            def _():
                pltpu.make_async_remote_copy(
                    src_ref=relay.at[n, j], dst_ref=rows.at[n, 0, p], send_sem=p_send.at[n],
                    recv_sem=p_recv.at[n], device_id=dev_owner(j), device_id_type=MESH,
                ).start()

            @pl.when(j == j_self)
            def _():
                pltpu.make_async_copy(relay.at[n, j], rows.at[n, 0, p], p_self.at[n]).start()

    def collected(n):
        wait_bytes(rows.at[n, 0, pl.ds(0, XY - 1)], p_recv.at[n])
        wait_bytes(rows.at[n, 0, 0], p_self.at[n])
        sib_copy(n).start()

    def own_ranks():
        wait_bytes(rp.at[pl.ds(0, XY - 1)], rp_recv)
        wait_bytes(rp.at[0], rp_self)
        for n in range(Z):
            total = rp[0, n]
            for q in range(1, XY):
                total = total + rp[q, n]
            rkown[n] = jnp.where(total > 0.5, total - 1.0, NONE_RANK)
            res[n] = jnp.full((1, W), -1.0, jnp.float32)
        rank_sib_copy().start()

    def rank_columns():
        rank_sib_copy().wait_recv()
        for half, ref in enumerate((rkown, rksib)):
            lined = jnp.concatenate(
                [ref[n] for n in range(Z)] + [jnp.zeros((128 - Z, W), jnp.float32)], axis=0
            )
            turned = lined.T
            for n in range(Z):
                rj[n, pl.ds(half * W, W), :] = jnp.broadcast_to(turned[:, n : n + 1], (W, 128))

    def pairs(m, n):
        other = rows[m].reshape(K * W, width)
        mine = rows[n, 0].reshape(W, width)
        scores = lax.dot_general(
            other, mine, (((1,), (1,)), ((), ())), preferred_element_type=jnp.float32
        )
        rank_i = rkown[n]
        rank_j = rj[m]
        best = []
        lanes = min(128, W)
        for at in range(0, W, lanes):
            earlier = rank_j[:, :lanes] < rank_i[:, at : at + lanes]
            kept = jnp.where(earlier, scores[:, at : at + lanes], -1.0)
            best.append(jnp.max(kept, axis=0, keepdims=True))
        res[n] = jnp.maximum(res[n], jnp.concatenate(best, axis=1))

    def compute(n):
        sib_copy(n).wait_recv()
        pairs(n, n)
        if n > 0:
            @pl.loop(0, n)
            def _(m):
                pairs(m, n)
                pairs(n, m)

    for n in range(Z):
        if n > 0:
            line_copy(n).wait_recv()
        forward(n)

        @pl.when(owner)
        def _(n=n):
            if n == 1:
                own_ranks()
            if n >= 1:
                collected(n - 1)
            if n == 2:
                rank_columns()
            if n >= 2:
                compute(n - 2)

    @pl.when(owner)
    def _():
        collected(Z - 1)
        compute(Z - 2)
        compute(Z - 1)

        @pl.loop(0, XY)
        def _(q):
            @pl.when(q != p)
            def _():
                pltpu.make_async_remote_copy(
                    src_ref=res, dst_ref=ret1.at[j_self], send_sem=r1_send, recv_sem=r1_recv,
                    device_id=dev_member(q), device_id_type=MESH,
                ).start()

        pltpu.make_async_copy(res, ret1.at[j_self], r1_self).start()
        wait_bytes(ret1.at[pl.ds(0, J - 1)], r1_recv)
        wait_bytes(ret1.at[0], r1_self)

    @pl.when(jnp.logical_not(owner))
    def _():
        wait_bytes(ret1, r1_recv)

    def home_copy(n):
        return pltpu.make_async_remote_copy(
            src_ref=ret1.at[:, n], dst_ref=ret2.at[n], send_sem=r2_send.at[n],
            recv_sem=r2_recv.at[n], device_id=dev_line(order[n]), device_id_type=MESH,
        )

    for n in range(1, Z):
        home_copy(n).start()

    for n in range(1, Z):
        rank_copy(n).wait_send()
        line_copy(n).wait_send()

    @pl.when(owner)
    def _():
        for n in range(Z):
            wait_bytes(relay.at[n, pl.ds(0, J - 1)], p_send.at[n])
            sib_copy(n).wait_send()
        wait_bytes(rp.at[pl.ds(0, J - 1)], rp_send)
        rank_sib_copy().wait_send()
        wait_bytes(rp.at[pl.ds(0, XY - 1)], r1_send)

    @pl.when(jnp.logical_not(owner))
    def _():
        for n in range(Z):
            wait_bytes(relay.at[n], p_send.at[n])
        wait_bytes(rp.at[pl.ds(0, J)], rp_send)

    for n in range(1, Z):
        home_copy(n).wait_recv()
    table = jnp.concatenate(
        [ret1[j, 0] for j in range(J)] + [ret2[n, j] for n in range(1, Z) for j in range(J)],
        axis=0,
    )
    hi = table.astype(jnp.bfloat16)
    rest = table - hi.astype(jnp.float32)
    mid = rest.astype(jnp.bfloat16)
    low = (rest - mid.astype(jnp.float32)).astype(jnp.bfloat16)
    found = jnp.zeros((W, n_docs), jnp.float32)
    for part in (low, mid, hi):
        found = found + lax.dot_general(
            part, hot[...], (((0,), (0,)), ((), ())), preferred_element_type=jnp.float32
        )
    out_ref[...] = jnp.sum(found * lane_hot[...].astype(jnp.float32), axis=0, keepdims=True)
    for n in range(1, Z):
        home_copy(n).wait_send()


def on_device(cfg, embeddings, doc_cluster, doc_rank):
    n_docs, width = embeddings.shape
    Z, J, W, XY, SLOT, K = cfg.Z, cfg.J, cfg.W, cfg.XY, cfg.SLOT, cfg.K
    bf16, f32 = jnp.bfloat16, jnp.float32
    dma = pltpu.SemaphoreType.DMA
    best = pl.pallas_call(
        functools.partial(kernel, cfg),
        out_shape=jax.ShapeDtypeStruct((1, n_docs), f32),
        in_specs=[pl.BlockSpec(memory_space=pltpu.VMEM)] * 3,
        out_specs=pl.BlockSpec(memory_space=pltpu.VMEM),
        scratch_shapes=[
            pltpu.VMEM((n_docs, width), bf16),
            pltpu.VMEM((Z * J, n_docs), bf16),
            pltpu.VMEM((W, n_docs), bf16),
            pltpu.VMEM((Z, J, SLOT, width), bf16),
            pltpu.VMEM((Z, J, SLOT, width), bf16),
            pltpu.VMEM((Z, K, XY, SLOT, width), bf16),
            pltpu.VMEM((Z, J, 1, W), f32),
            pltpu.VMEM((Z, J, 1, W), f32),
            pltpu.VMEM((XY, Z, 1, W), f32),
            pltpu.VMEM((Z, 1, W), f32),
            pltpu.VMEM((Z, 1, W), f32),
            pltpu.VMEM((Z, K * W, 128), f32),
            pltpu.VMEM((Z, 1, W), f32),
            pltpu.VMEM((J, Z, 1, W), f32),
            pltpu.VMEM((Z, J, 1, W), f32),
            dma((Z,)), dma((Z,)), dma((Z,)), dma((Z,)),
            dma((Z,)), dma((Z,)), dma((Z,)),
            dma, dma, dma,
            dma((Z,)), dma((Z,)), dma, dma,
            dma, dma, dma,
            dma((Z,)), dma((Z,)),
        ],
        compiler_params=pltpu.CompilerParams(
            collective_id=0, has_side_effects=True, vmem_limit_bytes=48 * 2**20
        ),
    )(embeddings, doc_cluster.reshape(1, n_docs), doc_rank.reshape(1, n_docs))
    return best.reshape(n_docs)


def solution(mesh):
    cfg = make_config(**SIZES)
    placed = (P(("shard", "rep"), None), P(("shard", "rep"), None), P(("shard", "rep")))
    return jax.shard_map(
        functools.partial(on_device, cfg), mesh=mesh, in_specs=placed,
        out_specs=P(("shard", "rep")), check_vma=False,
    )
```

time: 262 us -> 98.6 us (0.38); the launches traced: 258 us -> 98.4 us
  waiting for transfers between devices: 101 us -> 0 us
  Pallas kernels: 0 us -> 95.2 us
  matrix products: 35.5 us -> 0 us
  between operations: 33.9 us -> 0.01 us
  local copies, waits for them, and re-layouts: 32.4 us -> 3.17 us
  starting transfers between devices: 28 us -> 0 us
  other arithmetic: 14.6 us -> 0 us
  blocking collectives: 12.5 us -> 0 us
    pallas_call x0 -> x1, Pallas kernels: none -> 95.2 us  [on_device(): pl.pallas_call(functools.partial(kernel, cfg), out_shape=jax.ShapeDtypeSt...]
    all_to_all x3 -> x0, waiting for transfers between devices: 57.8 us -> none  [the longest x1 46.3 us: on_device(): lax.all_to_all(outgoing.reshape(owners, slots, width), 'shard', split_axi...]
    all_gather x1 -> x0, waiting for transfers between devices: 42.9 us -> none  [on_device(): piece_rows = lax.all_gather(packed, 'rep', axis=0, tiled=True)]
    dot_general x16 -> x0, matrix products: 35.5 us -> none  [compute_tile(): lax.dot_general(tile_rows, other_rows, (((1,), (1,)), ((), ())), preferre...]
    all_to_all x3 -> x0, starting transfers between devices: 28 us -> none  [the longest x1 11.6 us: on_device(): lax.all_to_all(out_rank.reshape(owners, slots), 'shard', split_axis=0, co...]
    scatter x3 -> x0, local copies, waits for them, and re-layouts: 13.8 us -> none  [the longest x1 6.88 us: on_device(): packed = jnp.zeros_like(member_rows).at[placement].set(member_rows)]
    all_gather x1 -> x0, blocking collectives: 12.5 us -> none  [on_device(): piece_rank = lax.all_gather(packed_rank, 'rep', axis=0, tiled=True)]
    gather x2 -> x0, local copies, waits for them, and re-layouts: 7.94 us -> none  [the longest x1 4.53 us: on_device(): slot_best = packed_best[placement].reshape(owners, slots)]
  transfers between devices with their start and end apart: 4 -> 0, of which waited for: 4 -> 0; matrix products, arithmetic and copies ran while one was open for 7% -> 0% of each run, Pallas kernels for 0% -> 0%
where the time goes in v1:
time: 98.6 us; the launch traced here: 98.4 us
  Pallas kernels  95.2 us (97%)
  local copies, waits for them, and re-layouts  3.17 us (3%)
    pallas_call x1, Pallas kernels, on_device(): pl.pallas_call(functools.partial(kernel, cfg), out_shape=jax.ShapeDtypeSt...  95.2 us
    unnamed x7, local copies, waits for them, and re-layouts  3.17 us

profile of v1, /device:TPU:32, one launch (start us, length us, event | category | flops | bytes accessed | tf_op | source)
XLA Modules:
  0.0 98.4 jit_solution(16337010074936059519)
XLA Ops:
  0.0 0.0 copy-start.1
  0.0 0.7 copy-done.1
  0.7 0.0 copy-start
  0.7 1.2 %copy-done = bf16[512,1024]{1,0:T(8,128)(2,1)S(1)} copy-done((bf16[512,1024]{1,0:T(8,128)(2,1)S(1)}, bf16[512,1024]{1,0:T(8,128)(2,1)}, u32[]{:S(2)}) %copy-start) | copy-done | bytes 1048600
  1.9 0.0 copy-start.2
  1.9 0.7 copy-done.2
  2.6 95.2 %shard_map.37 = f32[1,512]{1,0:T(1,128)S(1)} custom-call(bf16[512,1024]{1,0:T(8,128)(2,1)S(1)} %copy-done, s32[1,512]{1,0:T(1,128)S(1)} %bitcast.4, s32[1,512]{1,0:T(1,128)S(1)} %bitcast.5), custom_call_target="tpu_custom_call" | custom-call | tf_op jit(solution)/shard_map/pallas_call | solution.py:343
  97.8 0.6 copy.5
Async XLA Ops:
  0.0 0.7 copy-start.1
  0.7 1.2 %copy-start = (bf16[512,1024]{1,0:T(8,128)(2,1)S(1)}, bf16[512,1024]{1,0:T(8,128)(2,1)}, u32[]{:S(2)}) copy-start(bf16[512,1024]{1,0:T(8,128)(2,1)} %emb_ref.1) | copy-start | bytes 3145732
  1.9 0.7 copy-start.2

commit v2 on v1

v2 whole, which is shorter than its diff:
```python
import functools
from types import SimpleNamespace

import jax
import jax.numpy as jnp
from jax import lax
from jax.experimental import pallas as pl
from jax.experimental.pallas import tpu as pltpu
from jax.sharding import PartitionSpec as P

SIZES = dict(Z=8, X=4, Y=4, K=2, SLOT=16)
MESH = pl.DeviceIdType.MESH
NONE_RANK = 2.0e9


def make_config(Z, X, Y, K, SLOT):
    return SimpleNamespace(
        Z=Z, X=X, Y=Y, K=K, SLOT=SLOT, XY=X * Y, J=X * K, W=X * Y * SLOT, YS=Y // K, H=min(2, X * K),
        order=[0] + [d for i in range(1, Z // 2) for d in (i, Z - i)] + [Z // 2],
    )


def kernel(
    cfg, emb_hbm, cl_hbm, rank_hbm, out_ref,
    emb_ref, cl_ref, rank_ref, unit, row_hot, lane_hot, sbuf, relay, rows,
    rs, rz, rsum, rp, rkown, rksib, rj, res, msg, ret1, rback, ret2,
    in_sem, z_send, z_recv, rz_send, rz_recv, p_send, p_recv, p_self, rp_send, rp_recv, rp_self,
    s_send, s_recv, rks_send, rks_recv, r1_send, r1_recv, r1_self, r2_send, r2_recv,
):
    Z, X, Y, K, SLOT, XY, J, W, YS = (
        cfg.Z, cfg.X, cfg.Y, cfg.K, cfg.SLOT, cfg.XY, cfg.J, cfg.W, cfg.YS
    )
    order = cfg.order
    H = cfg.H
    JH = J // H
    n_docs, width = emb_ref.shape
    held = J * SLOT
    shard = lax.axis_index("shard")
    y = lax.axis_index("rep")
    k = shard % K
    x = (shard // K) % X
    z = shard // (K * X)
    p = x * Y + y
    owner = (y % YS) == (x % YS)
    j_self = jnp.where(owner, x * K + y // YS, -1)

    def dev(zz, xx, yy, kk):
        return ((zz * X + xx) * K + kk, yy)

    def dev_line(distance):
        return dev((z + distance) % Z, x, y, k)

    def dev_owner(j):
        xx = j // K
        return dev(z, xx, (j % K) * YS + xx % YS, k)

    def dev_member(q):
        return dev(z, q // Y, q % Y, k)

    sibling = dev(z, x, y, 1 - k)

    inputs = [
        pltpu.make_async_copy(src, dst, in_sem.at[i])
        for i, (src, dst) in enumerate(
            ((cl_hbm, cl_ref), (rank_hbm, rank_ref), (emb_hbm, emb_ref))
        )
    ]
    for copy in inputs:
        copy.start()

    barrier = pltpu.get_barrier_semaphore()

    @pl.loop(1, Z)
    def _(i):
        pl.semaphore_signal(barrier, inc=1, device_id=dev_line(i), device_id_type=MESH)

    @pl.loop(0, J)
    def _(j):
        @pl.when(j != j_self)
        def _():
            pl.semaphore_signal(barrier, inc=1, device_id=dev_owner(j), device_id_type=MESH)

    @pl.when(owner)
    def _():
        @pl.loop(0, XY)
        def _(q):
            @pl.when(q != p)
            def _():
                pl.semaphore_signal(barrier, inc=1, device_id=dev_member(q), device_id_type=MESH)

        pl.semaphore_signal(barrier, inc=1, device_id=sibling, device_id_type=MESH)

    inputs[0].wait()
    inputs[1].wait()
    cl = cl_ref[...]
    log_j = J.bit_length() - 1
    away = (z - (cl >> log_j)) & (Z - 1)
    step = jnp.where(away == 0, 0, jnp.where(away <= Z // 2, 2 * away - 1, 2 * (Z - away)))
    rel = step * J + (cl & (J - 1))
    member = lax.broadcasted_iota(jnp.int32, (Z * J, n_docs), 0) == rel
    hot_f = jnp.where(member, 1.0, 0.0)
    before = (
        lax.broadcasted_iota(jnp.int32, (n_docs, n_docs), 0)
        < lax.broadcasted_iota(jnp.int32, (n_docs, n_docs), 1)
    )
    prefix = jnp.dot(
        hot_f.astype(jnp.bfloat16), jnp.where(before, 1.0, 0.0).astype(jnp.bfloat16),
        preferred_element_type=jnp.float32,
    )
    seat = jnp.sum(hot_f * prefix, axis=0, keepdims=True).astype(jnp.int32)
    place = rel * SLOT + seat
    lane = (cl & (J - 1)) * SLOT + seat
    lane_b = jnp.where(
        lax.broadcasted_iota(jnp.int32, (held, n_docs), 0) == lane, 1.0, 0.0
    ).astype(jnp.bfloat16)
    lane_hot[...] = lane_b
    row_f = jnp.where(lax.broadcasted_iota(jnp.int32, (Z, n_docs), 0) == step, 1.0, 0.0)
    row_hot[...] = row_f

    rank1 = rank_ref[...] + 1
    parts = [(rank1 & 63), ((rank1 >> 6) & 63), (rank1 >> 12)]
    rank_rows = jnp.zeros((Z, held), jnp.float32)
    for weight, part in zip((1.0, 64.0, 4096.0), parts):
        rank_rows = rank_rows + weight * lax.dot_general(
            (row_f * part.astype(jnp.float32)).astype(jnp.bfloat16), lane_b,
            (((1,), (1,)), ((), ())), preferred_element_type=jnp.float32,
        )
    chunk_row = lax.broadcasted_iota(jnp.int32, (Z, held), 0)
    lane_group = lax.broadcasted_iota(jnp.int32, (Z, held), 1) // SLOT
    for n in range(Z):
        rs[n] = jnp.where(chunk_row == n, rank_rows, 0.0)

    inputs[2].wait()
    block = min(64, n_docs)

    @pl.loop(0, n_docs // block)
    def _(i):
        at = pl.ds(pl.multiple_of(i * block, block), block)
        values = emb_ref[at].astype(jnp.float32)
        scale = lax.rsqrt(jnp.sum(values * values, axis=1, keepdims=True) + 1e-06)
        unit[at] = (values * scale).astype(jnp.bfloat16)

    def pack(n):
        slots = lax.broadcasted_iota(jnp.int32, (J * SLOT, n_docs), 0) + n * J * SLOT
        pick = jnp.where(slots == place, 1.0, 0.0).astype(jnp.bfloat16)
        got = jnp.dot(pick, unit[...], preferred_element_type=jnp.float32)
        return got.astype(jnp.bfloat16).reshape(J, SLOT, width)

    def rank_copy(n):
        return pltpu.make_async_remote_copy(
            src_ref=rs.at[n], dst_ref=rz.at[n], send_sem=rz_send.at[n], recv_sem=rz_recv.at[n],
            device_id=dev_line(Z - order[n]), device_id_type=MESH,
        )

    def piece(h):
        return jnp.where(k == 0, h, H - 1 - h) * JH

    def line_copy(n, h):
        part = pl.ds(piece(h), JH)
        at = n * H + h
        return pltpu.make_async_remote_copy(
            src_ref=sbuf.at[n, part], dst_ref=relay.at[n, part], send_sem=z_send.at[at],
            recv_sem=z_recv.at[at], device_id=dev_line(Z - order[n]), device_id_type=MESH,
        )

    for n in range(1, Z):
        sbuf[n] = pack(n)
    relay[0] = pack(0)
    pl.semaphore_wait(
        barrier, jnp.where(owner, (Z - 1) + (J - 1) + (XY - 1) + 1, (Z - 1) + J)
    )

    for h in range(H):
        line_copy(1, h).start()
        line_copy(2, h).start()
    for n in range(1, Z):
        rank_copy(n).start()
    for n in range(3, Z, 2):
        for h in range(H):
            for step_n in range(n, min(n + 2, Z)):
                line_copy(step_n, h).start()

    def owner_turn(turn):
        return (x * K + y // YS + jnp.where(k == 0, turn, J - turn)) % J

    def wait_bytes(ref, sem):
        pltpu.make_async_copy(ref, ref, sem).wait()

    def sib_copy(n):
        return pltpu.make_async_remote_copy(
            src_ref=rows.at[n, 0], dst_ref=rows.at[n, 1], send_sem=s_send.at[n],
            recv_sem=s_recv.at[n], device_id=sibling, device_id_type=MESH,
        )

    def rank_sib_copy():
        return pltpu.make_async_remote_copy(
            src_ref=rkown, dst_ref=rksib, send_sem=rks_send, recv_sem=rks_recv,
            device_id=sibling, device_id_type=MESH,
        )

    def forward(n, h):
        @pl.loop(0, JH)
        def _(turn):
            j = piece(h) + (x * K + y // YS + turn) % JH

            @pl.when(j != j_self)
            def _():
                pltpu.make_async_remote_copy(
                    src_ref=relay.at[n, j], dst_ref=rows.at[n, 0, p], send_sem=p_send.at[n],
                    recv_sem=p_recv.at[n], device_id=dev_owner(j), device_id_type=MESH,
                ).start()

            @pl.when(j == j_self)
            def _():
                pltpu.make_async_copy(relay.at[n, j], rows.at[n, 0, p], p_self.at[n]).start()

    def forward_ranks():
        for n in range(1, Z):
            rank_copy(n).wait_recv()
        rsum[...] = rs[0] + sum(rz[n] for n in range(1, Z))

        @pl.loop(0, J)
        def _(turn):
            j = owner_turn(turn)

            @pl.when(j != j_self)
            def _():
                pltpu.make_async_remote_copy(
                    src_ref=rsum, dst_ref=rp.at[p], send_sem=rp_send, recv_sem=rp_recv,
                    device_id=dev_owner(j), device_id_type=MESH,
                ).start()

            @pl.when(j == j_self)
            def _():
                pltpu.make_async_copy(rsum, rp.at[p], rp_self).start()

    def collected(n):
        wait_bytes(rows.at[n, 0, pl.ds(0, XY - 1)], p_recv.at[n])
        wait_bytes(rows.at[n, 0, 0], p_self.at[n])
        sib_copy(n).start()

    groups = held // SLOT

    def own_ranks():
        wait_bytes(rp.at[pl.ds(0, XY - 1)], rp_recv)
        wait_bytes(rp.at[0], rp_self)
        for part in range(XY // groups):
            total = jnp.zeros((Z, held), jnp.float32)
            for g in range(groups):
                shift = ((g - j_self + groups) % groups) * SLOT
                turned = pltpu.roll(rp[part * groups + g], shift, 1)
                total = total + jnp.where(lane_group == g, turned, 0.0)
            rkown[:, pl.ds(part * held, held)] = jnp.where(total > 0.5, total - 1.0, NONE_RANK)
        res[...] = jnp.full((Z, W), -1.0, jnp.float32)
        rank_sib_copy().start()

    def rank_columns():
        rank_sib_copy().wait_recv()
        for half, ref in enumerate((rkown, rksib)):
            lined = jnp.concatenate(
                [ref[...], jnp.zeros((128 - Z, W), jnp.float32)], axis=0
            )
            turned = lined.T
            for n in range(Z):
                rj[n, pl.ds(half * W, W), :] = jnp.broadcast_to(turned[:, n : n + 1], (W, 128))

    def pairs(m, count, n):
        other = rows[pl.ds(m, count)].reshape(count * K * W, width)
        mine = rows[n, 0].reshape(W, width)
        scores = lax.dot_general(
            other, mine, (((1,), (1,)), ((), ())), preferred_element_type=jnp.float32
        )
        at = pl.ds(n, 1)
        rank_i = rkown[at, :]
        rank_j = rj[pl.ds(m, count)].reshape(count * K * W, 128)
        best = []
        lanes = min(128, W)
        for first in range(0, W, lanes):
            earlier = rank_j[:, :lanes] < rank_i[:, first : first + lanes]
            kept = jnp.where(earlier, scores[:, first : first + lanes], -1.0)
            best.append(jnp.max(kept, axis=0, keepdims=True))
        res[at, :] = jnp.maximum(res[at, :], jnp.concatenate(best, axis=1))

    def compute(n):
        sib_copy(n).wait_recv()
        if n > 1:
            @pl.loop(0, n // 2)
            def _(i):
                pairs(2 * i, 2, n)
                pairs(n, 1, 2 * i)
                pairs(n, 1, 2 * i + 1)
        if n % 2:
            pairs(n - 1, 2, n)
            pairs(n, 1, n - 1)
        else:
            pairs(n, 1, n)

    for n in range(Z):
        for h in range(H):
            if n > 0:
                line_copy(n, h).wait_recv()
            forward(n, h)
        if n == 0:
            forward_ranks()

        @pl.when(owner)
        def _(n=n):
            if n == 1:
                own_ranks()
            if n >= 1:
                collected(n - 1)
            if n == 2:
                rank_columns()
            if n >= 2:
                compute(n - 2)

    @pl.when(owner)
    def _():
        collected(Z - 1)
        compute(Z - 2)
        compute(Z - 1)

        for q in range(XY):
            shift = ((j_self - q) % groups) * SLOT
            half = res[:, pl.ds(q // groups * held, held)]
            msg[q] = jnp.where(lane_group == j_self, pltpu.roll(half, shift, 1), 0.0)

        @pl.loop(1, XY)
        def _(i):
            q = (p + i) % XY
            pltpu.make_async_remote_copy(
                src_ref=msg.at[q], dst_ref=ret1.at[j_self], send_sem=r1_send, recv_sem=r1_recv,
                device_id=dev_member(q), device_id_type=MESH,
            ).start()

        pltpu.make_async_copy(msg.at[p], ret1.at[j_self], r1_self).start()
        wait_bytes(ret1.at[pl.ds(0, J - 1)], r1_recv)
        wait_bytes(ret1.at[0], r1_self)

    @pl.when(jnp.logical_not(owner))
    def _():
        wait_bytes(ret1, r1_recv)

    rback[...] = sum(ret1[j] for j in range(1, J)) + ret1[0]

    def home_copy(n):
        return pltpu.make_async_remote_copy(
            src_ref=rback, dst_ref=ret2.at[n], send_sem=r2_send.at[n],
            recv_sem=r2_recv.at[n], device_id=dev_line(order[n]), device_id_type=MESH,
        )

    for n in range(1, Z):
        home_copy(n).start()

    for n in range(1, Z):
        rank_copy(n).wait_send()
        for h in range(H):
            line_copy(n, h).wait_send()

    @pl.when(owner)
    def _():
        for n in range(Z):
            wait_bytes(relay.at[n, pl.ds(0, J - 1)], p_send.at[n])
            sib_copy(n).wait_send()
        wait_bytes(rp.at[pl.ds(0, J - 1)], rp_send)
        rank_sib_copy().wait_send()
        wait_bytes(msg.at[pl.ds(0, XY - 1)], r1_send)

    @pl.when(jnp.logical_not(owner))
    def _():
        for n in range(Z):
            wait_bytes(relay.at[n], p_send.at[n])
        wait_bytes(rp.at[pl.ds(0, J)], rp_send)

    for n in range(1, Z):
        home_copy(n).wait_recv()
    table = jnp.where(chunk_row == 0, rback[...], 0.0)
    for n in range(1, Z):
        table = jnp.where(chunk_row == n, ret2[n], table)
    hi = table.astype(jnp.bfloat16).astype(jnp.float32)
    rest = table - hi
    mid = rest.astype(jnp.bfloat16).astype(jnp.float32)
    found = jnp.zeros((held, n_docs), jnp.float32)
    for part in (rest - mid, mid, hi):
        found = found + lax.dot_general(
            part.astype(jnp.bfloat16), row_hot[...].astype(jnp.bfloat16),
            (((0,), (0,)), ((), ())), preferred_element_type=jnp.float32,
        )
    out_ref[...] = jnp.sum(found * lane_hot[...].astype(jnp.float32), axis=0, keepdims=True)
    for n in range(1, Z):
        home_copy(n).wait_send()


def on_device(cfg, embeddings, doc_cluster, doc_rank):
    n_docs, width = embeddings.shape
    Z, J, W, XY, SLOT, K = cfg.Z, cfg.J, cfg.W, cfg.XY, cfg.SLOT, cfg.K
    bf16, f32 = jnp.bfloat16, jnp.float32
    dma = pltpu.SemaphoreType.DMA
    best = pl.pallas_call(
        functools.partial(kernel, cfg),
        out_shape=jax.ShapeDtypeStruct((1, n_docs), f32),
        in_specs=[pl.BlockSpec(memory_space=pl.ANY)] * 3,
        out_specs=pl.BlockSpec(memory_space=pltpu.VMEM),
        scratch_shapes=[
            pltpu.VMEM((n_docs, width), bf16),
            pltpu.VMEM((1, n_docs), jnp.int32),
            pltpu.VMEM((1, n_docs), jnp.int32),
            pltpu.VMEM((n_docs, width), bf16),
            pltpu.VMEM((Z, n_docs), f32),
            pltpu.VMEM((J * SLOT, n_docs), bf16),
            pltpu.VMEM((Z, J, SLOT, width), bf16),
            pltpu.VMEM((Z, J, SLOT, width), bf16),
            pltpu.VMEM((Z, K, XY, SLOT, width), bf16),
            pltpu.VMEM((Z, Z, J * SLOT), f32),
            pltpu.VMEM((Z, Z, J * SLOT), f32),
            pltpu.VMEM((Z, J * SLOT), f32),
            pltpu.VMEM((XY, Z, J * SLOT), f32),
            pltpu.VMEM((Z, W), f32),
            pltpu.VMEM((Z, W), f32),
            pltpu.VMEM((Z, K * W, 128), f32),
            pltpu.VMEM((Z, W), f32),
            pltpu.VMEM((XY, Z, J * SLOT), f32),
            pltpu.VMEM((J, Z, J * SLOT), f32),
            pltpu.VMEM((Z, J * SLOT), f32),
            pltpu.VMEM((Z, Z, J * SLOT), f32),
            dma((3,)),
            dma((Z * cfg.H,)), dma((Z * cfg.H,)), dma((Z,)), dma((Z,)),
            dma((Z,)), dma((Z,)), dma((Z,)),
            dma, dma, dma,
            dma((Z,)), dma((Z,)), dma, dma,
            dma, dma, dma,
            dma((Z,)), dma((Z,)),
        ],
        compiler_params=pltpu.CompilerParams(
            collective_id=0, has_side_effects=True, vmem_limit_bytes=63 * 2**20
        ),
    )(embeddings, doc_cluster.reshape(1, n_docs), doc_rank.reshape(1, n_docs))
    return best.reshape(n_docs)


def solution(mesh):
    cfg = make_config(**SIZES)
    placed = (P(("shard", "rep"), None), P(("shard", "rep"), None), P(("shard", "rep")))
    return jax.shard_map(
        functools.partial(on_device, cfg), mesh=mesh, in_specs=placed,
        out_specs=P(("shard", "rep")), check_vma=False,
    )
```

time: 98.6 us -> 91.6 us (0.929)
  Pallas kernels: 95.2 us -> 89.2 us
  local copies, waits for them, and re-layouts: 3.17 us -> 1.26 us
    pallas_call x1, Pallas kernels: 95.2 us -> 89.2 us  [on_device(): pl.pallas_call(functools.partial(kernel, cfg), out_shape=jax.ShapeDtypeSt...]
    unnamed x7 -> x1, local copies, waits for them, and re-layouts: 3.17 us -> 1.26 us
where the time goes in v2:
time: 91.6 us; the launch traced here: 90.4 us
  Pallas kernels  89.2 us (97%)
  local copies, waits for them, and re-layouts  1.26 us (1%)
    pallas_call x1, Pallas kernels, on_device(): pl.pallas_call(functools.partial(kernel, cfg), out_shape=jax.ShapeDtypeSt...  89.2 us

profile of v2, /device:TPU:32, one launch (start us, length us, event | category | flops | bytes accessed | tf_op | source)
XLA Modules:
  0.0 90.4 jit_solution(2605983140082051478)
XLA Ops:
  0.0 89.2 %shard_map.37 = f32[1,512]{1,0:T(1,128)} custom-call(bf16[512,1024]{1,0:T(8,128)(2,1)} %emb_hbm.1, s32[1,512]{1,0:T(1,128)} %bitcast.4, s32[1,512]{1,0:T(1,128)} %bitcast.5), custom_call_target="tpu_custom_call" | custom-call | tf_op jit(solution)/shard_map/pallas_call | solution.py:399
  89.2 1.3 %copy.5 = f32[512]{0:T(512)} copy(f32[512]{0:T(512)} %bitcast.3) | data formatting | bytes 4096

commit v3 on v2

--- a/solution.py
+++ b/solution.py
@@ -15,7 +15,7 @@
 
 def make_config(Z, X, Y, K, SLOT):
     return SimpleNamespace(
-        Z=Z, X=X, Y=Y, K=K, SLOT=SLOT, XY=X * Y, J=X * K, W=X * Y * SLOT, YS=Y // K, H=min(2, X * K),
+        Z=Z, X=X, Y=Y, K=K, SLOT=SLOT, XY=X * Y, J=X * K, W=X * Y * SLOT, YS=Y // K, H=4,
         order=[0] + [d for i in range(1, Z // 2) for d in (i, Z - i)] + [Z // 2],
     )
 
@@ -153,7 +153,7 @@
         )
 
     def piece(h):
-        return jnp.where(k == 0, h, H - 1 - h) * JH
+        return ((x * H // X + jnp.where(k == 0, h, H - h)) % H) * JH
 
     def line_copy(n, h):
         part = pl.ds(piece(h), JH)

time: 91.6 us -> 88.3 us (0.964)
  Pallas kernels: 89.2 us -> 86.2 us
    pallas_call x1, Pallas kernels: 89.2 us -> 86.2 us  [on_device(): pl.pallas_call(functools.partial(kernel, cfg), out_shape=jax.ShapeDtypeSt...]
where the time goes in v3:
time: 88.3 us; the launch traced here: 87.5 us
  Pallas kernels  86.2 us (98%)
  local copies, waits for them, and re-layouts  1.26 us (1%)
    pallas_call x1, Pallas kernels, on_device(): pl.pallas_call(functools.partial(kernel, cfg), out_shape=jax.ShapeDtypeSt...  86.2 us

profile of v3, /device:TPU:32, one launch (start us, length us, event | category | flops | bytes accessed | tf_op | source)
XLA Modules:
  0.0 87.5 jit_solution(2403226988253211146)
XLA Ops:
  0.0 86.2 %shard_map.37 = f32[1,512]{1,0:T(1,128)} custom-call(bf16[512,1024]{1,0:T(8,128)(2,1)} %emb_hbm.1, s32[1,512]{1,0:T(1,128)} %bitcast.4, s32[1,512]{1,0:T(1,128)} %bitcast.5), custom_call_target="tpu_custom_call" | custom-call | tf_op jit(solution)/shard_map/pallas_call | solution.py:399
  86.2 1.3 %copy.5 = f32[512]{0:T(512)} copy(f32[512]{0:T(512)} %bitcast.3) | data formatting | bytes 4096

commit v4 on v3

--- a/solution.py
+++ b/solution.py
@@ -281,25 +281,30 @@
             best.append(jnp.max(kept, axis=0, keepdims=True))
         res[at, :] = jnp.maximum(res[at, :], jnp.concatenate(best, axis=1))
 
-    def compute(n):
-        sib_copy(n).wait_recv()
-        if n > 1:
-            @pl.loop(0, n // 2)
-            def _(i):
-                pairs(2 * i, 2, n)
-                pairs(n, 1, 2 * i)
-                pairs(n, 1, 2 * i + 1)
-        if n % 2:
-            pairs(n - 1, 2, n)
-            pairs(n, 1, n - 1)
-        else:
-            pairs(n, 1, n)
+    def tasks(n):
+        calls = []
+        for m in range(0, n - 1, 2):
+            calls += [(m, 2, n), (n, 1, m), (n, 1, m + 1)]
+        calls += [(n - 1, 2, n), (n, 1, n - 1)] if n % 2 else [(n, 1, n)]
+        return calls
+
+    def compute(n, calls):
+        for call in calls:
+            pairs(*call)
 
     for n in range(Z):
+        waiting = tasks(n - 3) if n >= 3 else []
+        waiting = waiting[len(waiting) * 1 // 5 :]
         for h in range(H):
             if n > 0:
                 line_copy(n, h).wait_recv()
             forward(n, h)
+            now = waiting[h * len(waiting) // H : (h + 1) * len(waiting) // H]
+            if now:
+                @pl.when(owner)
+                def _(n=n, now=now):
+                    compute(n - 3, now)
+
         if n == 0:
             forward_ranks()
 
@@ -312,21 +317,26 @@
             if n == 2:
                 rank_columns()
             if n >= 2:
-                compute(n - 2)
+                sib_copy(n - 2).wait_recv()
+                calls = tasks(n - 2)
+                if n < Z - 1:
+                    calls = calls[: len(calls) * 1 // 5]
+                compute(n - 2, calls)
 
     @pl.when(owner)
     def _():
         collected(Z - 1)
-        compute(Z - 2)
-        compute(Z - 1)
+        sib_copy(Z - 2).wait_recv()
+        compute(Z - 2, tasks(Z - 2))
+        sib_copy(Z - 1).wait_recv()
+        compute(Z - 1, tasks(Z - 1))
 
         for q in range(XY):
             shift = ((j_self - q) % groups) * SLOT
             half = res[:, pl.ds(q // groups * held, held)]
             msg[q] = jnp.where(lane_group == j_self, pltpu.roll(half, shift, 1), 0.0)
 
-        @pl.loop(1, XY)
-        def _(i):
+        for i in range(1, XY):
             q = (p + i) % XY
             pltpu.make_async_remote_copy(
                 src_ref=msg.at[q], dst_ref=ret1.at[j_self], send_sem=r1_send, recv_sem=r1_recv,

time: 88.3 us -> 86.6 us (0.981)
  Pallas kernels: 86.2 us -> 84.8 us
    pallas_call x1, Pallas kernels: 86.2 us -> 84.8 us  [on_device(): pl.pallas_call(functools.partial(kernel, cfg), out_shape=jax.ShapeDtypeSt...]
where the time goes in v4:
time: 86.6 us; the launch traced here: 86.1 us
  Pallas kernels  84.8 us (98%)
  local copies, waits for them, and re-layouts  1.26 us (1%)
    pallas_call x1, Pallas kernels, on_device(): pl.pallas_call(functools.partial(kernel, cfg), out_shape=jax.ShapeDtypeSt...  84.8 us

profile of v4, /device:TPU:32, one launch (start us, length us, event | category | flops | bytes accessed | tf_op | source)
XLA Modules:
  0.0 86.1 jit_solution(4350300047600463724)
XLA Ops:
  0.0 84.8 %shard_map.37 = f32[1,512]{1,0:T(1,128)} custom-call(bf16[512,1024]{1,0:T(8,128)(2,1)} %emb_hbm.1, s32[1,512]{1,0:T(1,128)} %bitcast.4, s32[1,512]{1,0:T(1,128)} %bitcast.5), custom_call_target="tpu_custom_call" | custom-call | tf_op jit(solution)/shard_map/pallas_call | solution.py:409
  84.8 1.3 %copy.5 = f32[512]{0:T(512)} copy(f32[512]{0:T(512)} %bitcast.3) | data formatting | bytes 4096

commit v5 on v4

--- a/solution.py
+++ b/solution.py
@@ -294,7 +294,7 @@
 
     for n in range(Z):
         waiting = tasks(n - 3) if n >= 3 else []
-        waiting = waiting[len(waiting) * 1 // 5 :]
+        waiting = waiting[len(waiting) * 0 // 5 :]
         for h in range(H):
             if n > 0:
                 line_copy(n, h).wait_recv()
@@ -320,7 +320,7 @@
                 sib_copy(n - 2).wait_recv()
                 calls = tasks(n - 2)
                 if n < Z - 1:
-                    calls = calls[: len(calls) * 1 // 5]
+                    calls = calls[: len(calls) * 0 // 5]
                 compute(n - 2, calls)
 
     @pl.when(owner)

time: 86.6 us -> 86.2 us (level)
  no operation moved by 1% of the time
where the time goes in v5:
time: 86.2 us; the launch traced here: 86.1 us
  Pallas kernels  84.8 us (98%)
  local copies, waits for them, and re-layouts  1.26 us (1%)
    pallas_call x1, Pallas kernels, on_device(): pl.pallas_call(functools.partial(kernel, cfg), out_shape=jax.ShapeDtypeSt...  84.8 us

profile of v5, /device:TPU:32, one launch (start us, length us, event | category | flops | bytes accessed | tf_op | source)
XLA Modules:
  0.0 86.1 jit_solution(7341799999579104055)
XLA Ops:
  0.0 84.8 %shard_map.37 = f32[1,512]{1,0:T(1,128)} custom-call(bf16[512,1024]{1,0:T(8,128)(2,1)} %emb_hbm.1, s32[1,512]{1,0:T(1,128)} %bitcast.4, s32[1,512]{1,0:T(1,128)} %bitcast.5), custom_call_target="tpu_custom_call" | custom-call | tf_op jit(solution)/shard_map/pallas_call | solution.py:409
  84.8 1.3 %copy.5 = f32[512]{0:T(512)} copy(f32[512]{0:T(512)} %bitcast.3) | data formatting | bytes 4096
